TPU v7x, 256 devices: a whole 4x4x8 slice. The times are simulated.
256 devices in a mesh: ctx: 64 (over y, x, z_hi, core), tp: 4 (over z_lo).
Axes of the slice: x: 4, y: 4, z: 8 (z_hi: 2, z_lo: 4; z = z_hi * 4 + z_lo), core: 2. Of those that a mesh axis runs over, the one named last changes fastest.
Arguments:
- q_field: bfloat16 [4096, 16384], P('tp', 'ctx'), may hold values from -6 to 6
- k_field: bfloat16 [4096, 16384], P('tp', 'ctx'), may hold values from -6 to 6
- v_field: bfloat16 [4096, 16384], P('tp', 'ctx'), may hold values from -6 to 6
- out_grad: bfloat16 [4096, 16384], P('tp', 'ctx'), may hold values from -6 to 6
- filter_taps: float32 [4096, 16384], P('tp', 'ctx'), may hold values from -6 to 6
- skip: float32 [4096], P('tp'), may hold values from 0.5 to 1.5
Outputs:
- q_grad: bfloat16 [4096, 16384], P('tp', 'ctx')
- k_grad: bfloat16 [4096, 16384], P('tp', 'ctx')
- v_grad: bfloat16 [4096, 16384], P('tp', 'ctx')
- filter_grad: float32 [4096, 16384], P('tp', 'ctx')
All inputs are finite; a program needn't handle non-finite values.
Results may differ from a plain program's by a relative error of at most 0.012.
Values may be sent and summed in bfloat16 or wider, within the bound.
A program may use at most 128 MiB of HBM per device.

v0:
```python
import math

import jax
import jax.numpy as jnp
from jax import lax
from jax.sharding import PartitionSpec as P

highest = lax.Precision.HIGHEST


def angle_table(rows, cols, modulus):
    row_index = lax.iota(jnp.int32, rows)[:, None]
    col_index = lax.iota(jnp.int32, cols)[None, :]
    angle = (row_index * col_index % modulus).astype(jnp.float32) * (2.0 * math.pi / modulus)
    return (jnp.cos(angle), jnp.sin(angle))


def forward_transform(signal, tables):
    cosine_rows, sine_rows, twist_cos, twist_sin, cosine_cols, sine_cols = tables
    channels = signal.shape[0]
    grid = signal.reshape(channels, cosine_rows.shape[0], cosine_cols.shape[0])
    first_real = jnp.einsum("ca,zab->zcb", cosine_rows, grid, precision=highest)
    first_imag = -jnp.einsum("ca,zab->zcb", sine_rows, grid, precision=highest)
    turned_real = first_real * twist_cos + first_imag * twist_sin
    turned_imag = first_imag * twist_cos - first_real * twist_sin
    spec_real = jnp.einsum("zcb,bd->zcd", turned_real, cosine_cols, precision=highest) + jnp.einsum(
        "zcb,bd->zcd", turned_imag, sine_cols, precision=highest
    )
    spec_imag = jnp.einsum("zcb,bd->zcd", turned_imag, cosine_cols, precision=highest) - jnp.einsum(
        "zcb,bd->zcd", turned_real, sine_cols, precision=highest
    )
    return (spec_real, spec_imag)


def inverse_transform(spec_real, spec_imag, tables, length):
    cosine_rows, sine_rows, twist_cos, twist_sin, cosine_cols, sine_cols = tables
    channels = spec_real.shape[0]
    n_len = cosine_rows.shape[0] * cosine_cols.shape[0]
    mid_real = jnp.einsum("zcd,db->zcb", spec_real, cosine_cols, precision=highest) - jnp.einsum(
        "zcd,db->zcb", spec_imag, sine_cols, precision=highest
    )
    mid_imag = jnp.einsum("zcd,db->zcb", spec_imag, cosine_cols, precision=highest) + jnp.einsum(
        "zcd,db->zcb", spec_real, sine_cols, precision=highest
    )
    turned_real = mid_real * twist_cos - mid_imag * twist_sin
    turned_imag = mid_imag * twist_cos + mid_real * twist_sin
    signal = jnp.einsum("ac,zcb->zab", cosine_rows, turned_real, precision=highest) - jnp.einsum(
        "ac,zcb->zab", sine_rows, turned_imag, precision=highest
    )
    return (signal / n_len).reshape(channels, n_len)[:, :length]


def convolve_fields(gated, product, taps):
    length = gated.shape[1]
    n_len = 2 * length
    cols = 128
    rows = n_len // cols
    cosine_rows, sine_rows = angle_table(rows, rows, rows)
    twist_cos, twist_sin = angle_table(rows, cols, n_len)
    cosine_cols, sine_cols = angle_table(cols, cols, cols)
    tables = (cosine_rows, sine_rows, twist_cos, twist_sin, cosine_cols, sine_cols)
    padding = ((0, 0), (0, length))
    gated_real, gated_imag = forward_transform(jnp.pad(gated.astype(jnp.float32), padding), tables)
    product_real, product_imag = forward_transform(
        jnp.pad(product.astype(jnp.float32), padding), tables
    )
    taps_real, taps_imag = forward_transform(jnp.pad(taps, padding), tables)
    forward = inverse_transform(
        gated_real * taps_real - gated_imag * taps_imag,
        gated_real * taps_imag + gated_imag * taps_real,
        tables,
        length,
    )
    backward = inverse_transform(
        product_real * taps_real + product_imag * taps_imag,
        product_imag * taps_real - product_real * taps_imag,
        tables,
        length,
    )
    taps_grad = inverse_transform(
        product_real * gated_real + product_imag * gated_imag,
        product_imag * gated_real - product_real * gated_imag,
        tables,
        length,
    )
    return (forward, backward, taps_grad * length ** (-0.5))


def finish_grads(k_part, v_part, grad_part, gated, product, forward_b, backward_b, skip_col):
    conv_total = forward_b.astype(jnp.float32) + skip_col * gated.astype(jnp.float32)
    q_grad = (grad_part.astype(jnp.float32) * conv_total).astype(jnp.bfloat16)
    z_grad = backward_b.astype(jnp.float32) + skip_col * product.astype(jnp.float32)
    k_grad = (v_part.astype(jnp.float32) * z_grad).astype(jnp.bfloat16)
    v_grad = (k_part.astype(jnp.float32) * z_grad).astype(jnp.bfloat16)
    return (q_grad, k_grad, v_grad)


def local(q_field, k_field, v_field, out_grad, filter_taps, skip):
    taps = lax.all_to_all(filter_taps, "ctx", split_axis=0, concat_axis=1, tiled=True)
    q_chan, k_chan, v_chan, grad_chan = (
        lax.all_to_all(q_field, "ctx", split_axis=0, concat_axis=1, tiled=True),
        lax.all_to_all(k_field, "ctx", split_axis=0, concat_axis=1, tiled=True),
        lax.all_to_all(v_field, "ctx", split_axis=0, concat_axis=1, tiled=True),
        lax.all_to_all(out_grad, "ctx", split_axis=0, concat_axis=1, tiled=True),
    )
    gated = (k_chan.astype(jnp.float32) * v_chan.astype(jnp.float32)).astype(jnp.bfloat16)
    product = (grad_chan.astype(jnp.float32) * q_chan.astype(jnp.float32)).astype(jnp.bfloat16)
    forward, backward, taps_grad = convolve_fields(gated, product, taps)
    count = gated.shape[0]
    local_skip = lax.dynamic_slice_in_dim(skip, lax.axis_index("ctx") * count, count)[:, None]
    forward_b = lax.optimization_barrier(forward.astype(jnp.bfloat16))
    backward_b = lax.optimization_barrier(backward.astype(jnp.bfloat16))
    grads_chan = finish_grads(
        k_chan, v_chan, grad_chan, gated, product, forward_b, backward_b, local_skip
    )
    q_grad, k_grad, v_grad = (
        lax.all_to_all(grads_chan[0], "ctx", split_axis=1, concat_axis=0, tiled=True),
        lax.all_to_all(grads_chan[1], "ctx", split_axis=1, concat_axis=0, tiled=True),
        lax.all_to_all(grads_chan[2], "ctx", split_axis=1, concat_axis=0, tiled=True),
    )
    taps_out = lax.all_to_all(taps_grad, "ctx", split_axis=1, concat_axis=0, tiled=True)
    return (q_grad, k_grad, v_grad, taps_out)


def solution(mesh):
    return jax.shard_map(
        local,
        mesh=mesh,
        in_specs=(
            P("tp", "ctx"),
            P("tp", "ctx"),
            P("tp", "ctx"),
            P("tp", "ctx"),
            P("tp", "ctx"),
            P("tp"),
        ),
        out_specs=(P("tp", "ctx"), P("tp", "ctx"), P("tp", "ctx"), P("tp", "ctx")),
        check_vma=False,
    )
```

profile of v0, /device:TPU:33, one launch (start us, length us, event | category | flops | bytes accessed | tf_op | source)
XLA Modules:
  0.0 362.2 jit_solution(6126034371413498944)
XLA Ops:
  0.6 36.3 %all_to_all.147 = bf16[64,16,256]{2,1,0:T(8,128)(2,1)S(1)} all-to-all(bf16[64,16,256]{2,1,0:T(8,128)(2,1)} %bitcast.276), channel_id=1, replica_groups=mesh['ctx'=64,'tp'=4] {'ctx'}, dimensions={0} | all-to-all | bytes 1048576 | tf_op jit(solution)/shard_map/all_to_all | solution.py:102
  37.0 23.7 %all_to_all.148 = bf16[64,16,256]{2,1,0:T(8,128)(2,1)S(1)} all-to-all(bf16[64,16,256]{2,1,0:T(8,128)(2,1)} %bitcast.277), channel_id=1, replica_groups=mesh['ctx'=64,'tp'=4] {'ctx'}, dimensions={0} | all-to-all | bytes 1048576 | tf_op jit(solution)/shard_map/all_to_all | solution.py:103
  60.7 22.4 %all_to_all.149 = bf16[64,16,256]{2,1,0:T(8,128)(2,1)S(1)} all-to-all(bf16[64,16,256]{2,1,0:T(8,128)(2,1)S(1)} %bitcast.278), channel_id=1, replica_groups=mesh['ctx'=64,'tp'=4] {'ctx'}, dimensions={0} | all-to-all | bytes 1048576 | tf_op jit(solution)/shard_map/all_to_all | solution.py:104
  83.1 4.5 %all-to-all-start.5 = ((bf16[64,16,256]{2,1,0:T(8,128)(2,1)}), bf16[64,16,256]{2,1,0:T(8,128)(2,1)S(1)}, u32[]{:S(2)}, u32[]{:S(2)}) async-start(bf16[64,16,256]{2,1,0:T(8,128)(2,1)} %bitcast.19), calls=%async_computation.5 | async-start | bytes 1048576 | tf_op jit(solution)/shard_map/all_to_all | solution.py:101
  90.8 15.0 %all-to-all-done.5 = bf16[64,16,256]{2,1,0:T(8,128)(2,1)S(1)} async-done(((bf16[64,16,256]{2,1,0:T(8,128)(2,1)}), bf16[64,16,256]{2,1,0:T(8,128)(2,1)S(1)}, u32[]{:S(2)}, u32[]{:S(2)}) %all-to-all-start.5) | async-done | bytes 524320 | tf_op jit(solution)/shard_map/all_to_all | solution.py:101
  105.8 5.8 %all-to-all-start.3 = ((f32[64,16,256]{2,1,0:T(8,128)}), f32[64,16,256]{2,1,0:T(8,128)}, u32[]{:S(2)}, u32[]{:S(2)}) async-start(f32[64,16,256]{2,1,0:T(8,128)} %bitcast.275), calls=%async_computation.3 | async-start | bytes 2097152 | tf_op jit(solution)/shard_map/all_to_all | solution.py:99
  113.7 4.5 %fusion.84 = f32[16,128,256]{2,1,0:T(8,128)S(1)} fusion(f32[16,256,128]{2,1,0:T(8,128)S(1)} %bitcast.245), kind=kOutput, calls=%fused_computation.119 | convolution fusion | flops 1611530240 | bytes 4194304 | tf_op jit(solution)/shard_map/ca,zab->zcb/dot_general | solution.py:23
  118.1 4.5 %fusion.93 = f32[16,128,256]{2,1,0:T(8,128)S(1)} fusion(f32[16,256,128]{2,1,0:T(8,128)S(1)} %bitcast.246), kind=kOutput, calls=%fused_computation.128 | convolution fusion | flops 1611530240 | bytes 4194304 | tf_op jit(solution)/shard_map/ca,zab->zcb/dot_general | solution.py:22
  122.6 4.1 %fusion.56 = f32[16,256,128]{2,1,0:T(8,128)S(1)} fusion(f32[16,128,256]{2,1,0:T(8,128)S(1)} %fusion.93, f32[16,128,256]{2,1,0:T(8,128)S(1)} %fusion.84, f32[256,128]{0,1:T(8,128)S(1)} %get-tuple-element.17, f32[256,128]{0,1:T(8,128)S(1)} %get-tuple-element.18), kind=kOutput, calls=%fused_computation.100 | convolution fusion | flops 807632896 | bytes 6553600 | tf_op jit(solution)/shard_map/zcb,bd->zcd/dot_general | solution.py:29
  126.7 3.9 %fusion.60 = f32[16,256,128]{2,1,0:T(8,128)S(1)} fusion(f32[16,128,256]{2,1,0:T(8,128)S(1)} %fusion.93, f32[16,128,256]{2,1,0:T(8,128)S(1)} %fusion.84, f32[256,128]{0,1:T(8,128)S(1)} %get-tuple-element.17, f32[256,128]{0,1:T(8,128)S(1)} %get-tuple-element.18), kind=kOutput, calls=%fused_computation.101 | convolution fusion | flops 807632896 | bytes 6553600 | tf_op jit(solution)/shard_map/zcb,bd->zcd/dot_general | solution.py:26
  131.1 4.5 %fusion.79 = f32[16,128,256]{2,1,0:T(8,128)S(1)} fusion(f32[16,256,128]{2,1,0:T(8,128)S(1)} %bitcast.247), kind=kOutput, calls=%fused_computation.114 | convolution fusion | flops 1611530240 | bytes 4194304 | tf_op jit(solution)/shard_map/ca,zab->zcb/dot_general | solution.py:23
  135.6 4.7 %fusion.88 = f32[16,128,256]{2,1,0:T(8,128)S(1)} fusion(f32[16,256,128]{2,1,0:T(8,128)S(1)} %bitcast.248), kind=kOutput, calls=%fused_computation.123 | convolution fusion | flops 1611530240 | bytes 4194304 | tf_op jit(solution)/shard_map/ca,zab->zcb/dot_general | solution.py:22
  140.3 3.8 %fusion.68 = f32[16,256,128]{2,1,0:T(8,128)S(1)} fusion(f32[16,128,256]{2,1,0:T(8,128)S(1)} %fusion.88, f32[16,128,256]{2,1,0:T(8,128)S(1)} %fusion.79, f32[256,128]{0,1:T(8,128)S(1)} %get-tuple-element.17, f32[256,128]{0,1:T(8,128)S(1)} %get-tuple-element.18), kind=kOutput, calls=%fused_computation.104 | convolution fusion | flops 807632896 | bytes 6553600 | tf_op jit(solution)/shard_map/zcb,bd->zcd/dot_general | solution.py:29
  144.2 5.2 %fusion.72 = f32[16,256,128]{2,1,0:T(8,128)} fusion(f32[16,128,256]{2,1,0:T(8,128)S(1)} %fusion.88, f32[16,128,256]{2,1,0:T(8,128)S(1)} %fusion.79, f32[256,128]{0,1:T(8,128)S(1)} %get-tuple-element.17, f32[256,128]{0,1:T(8,128)S(1)} %get-tuple-element.18), kind=kOutput, calls=%fused_computation.105 | convolution fusion | flops 807632896 | bytes 6553600 | tf_op jit(solution)/shard_map/zcb,bd->zcd/dot_general | solution.py:26
  149.3 5.6 %convolution_subtract_fusion.5 = f32[16,256,128]{2,1,0:T(8,128)} fusion(f32[16,256,128]{2,1,0:T(8,128)S(1)} %fusion.56, f32[16,128,256]{2,1,0:T(8,128)S(1)} %fusion.93, f32[16,128,256]{2,1,0:T(8,128)S(1)} %fusion.84, f32[256,128]{0,1:T(8,128)S(1)} %get-tuple-element.17, f32[256,128]{0,1:T(8,128)S(1)} %get-tuple-element.18), kind=kOutput, calls=%fused_computation.64 | convolution fusion | flops 808157184 | bytes 8650752 | tf_op jit(solution)/shard_map/zcb,bd->zcd/dot_general | solution.py:29
  154.9 5.2 %convolution_add_fusion.5 = f32[16,256,128]{2,1,0:T(8,128)} fusion(f32[16,256,128]{2,1,0:T(8,128)S(1)} %fusion.60, f32[16,128,256]{2,1,0:T(8,128)S(1)} %fusion.93, f32[16,128,256]{2,1,0:T(8,128)S(1)} %fusion.84, f32[256,128]{0,1:T(8,128)S(1)} %get-tuple-element.17, f32[256,128]{0,1:T(8,128)S(1)} %get-tuple-element.18), kind=kOutput, calls=%fused_computation.66 | convolution fusion | flops 808157184 | bytes 8650752 | tf_op jit(solution)/shard_map/zcb,bd->zcd/dot_general | solution.py:26
  160.1 5.2 %convolution_subtract_fusion.2 = f32[16,256,128]{2,1,0:T(8,128)} fusion(f32[16,256,128]{2,1,0:T(8,128)S(1)} %fusion.68, f32[16,128,256]{2,1,0:T(8,128)S(1)} %fusion.88, f32[16,128,256]{2,1,0:T(8,128)S(1)} %fusion.79, f32[256,128]{0,1:T(8,128)S(1)} %get-tuple-element.17, f32[256,128]{0,1:T(8,128)S(1)} %get-tuple-element.18), kind=kOutput, calls=%fused_computation.59 | convolution fusion | flops 808157184 | bytes 8650752 | tf_op jit(solution)/shard_map/zcb,bd->zcd/dot_general | solution.py:29
  167.2 4.6 %fusion.82 = f32[16,128,256]{2,1,0:T(8,128)S(1)} fusion(f32[16,256,128]{2,1,0:T(8,128)S(1)} %bitcast.249), kind=kOutput, calls=%fused_computation.117 | convolution fusion | flops 1611530240 | bytes 4194304 | tf_op jit(solution)/shard_map/ca,zab->zcb/dot_general | solution.py:23
  171.9 4.5 %fusion.91 = f32[16,128,256]{2,1,0:T(8,128)S(1)} fusion(f32[16,256,128]{2,1,0:T(8,128)S(1)} %bitcast.250), kind=kOutput, calls=%fused_computation.126 | convolution fusion | flops 1611530240 | bytes 4194304 | tf_op jit(solution)/shard_map/ca,zab->zcb/dot_general | solution.py:22
  176.4 3.9 %fusion.62 = f32[16,256,128]{2,1,0:T(8,128)S(1)} fusion(f32[16,128,256]{2,1,0:T(8,128)S(1)} %fusion.91, f32[16,128,256]{2,1,0:T(8,128)S(1)} %fusion.82, f32[256,128]{0,1:T(8,128)S(1)} %get-tuple-element.17, f32[256,128]{0,1:T(8,128)S(1)} %get-tuple-element.18), kind=kOutput, calls=%fused_computation.102 | convolution fusion | flops 807632896 | bytes 6553600 | tf_op jit(solution)/shard_map/zcb,bd->zcd/dot_general | solution.py:29
  180.3 4.3 %fusion.66 = f32[16,256,128]{2,1,0:T(8,128)S(1)} fusion(f32[16,128,256]{2,1,0:T(8,128)S(1)} %fusion.91, f32[16,128,256]{2,1,0:T(8,128)S(1)} %fusion.82, f32[256,128]{0,1:T(8,128)S(1)} %get-tuple-element.17, f32[256,128]{0,1:T(8,128)S(1)} %get-tuple-element.18), kind=kOutput, calls=%fused_computation.103 | convolution fusion | flops 807632896 | bytes 6553600 | tf_op jit(solution)/shard_map/zcb,bd->zcd/dot_general | solution.py:26
  184.6 3.9 %convolution_subtract_fusion.4 = f32[16,256,128]{2,1,0:T(8,128)S(1)} fusion(f32[16,256,128]{2,1,0:T(8,128)S(1)} %fusion.62, f32[16,128,256]{2,1,0:T(8,128)S(1)} %fusion.91, f32[16,128,256]{2,1,0:T(8,128)S(1)} %fusion.82, f32[256,128]{0,1:T(8,128)S(1)} %get-tuple-element.17, f32[256,128]{0,1:T(8,128)S(1)} %get-tuple-element.18), kind=kOutput, calls=%fused_computation.63 | convolution fusion | flops 808157184 | bytes 8650752 | tf_op jit(solution)/shard_map/zcb,bd->zcd/dot_general | solution.py:29
  188.5 3.9 %convolution_add_fusion.4 = f32[16,256,128]{2,1,0:T(8,128)S(1)} fusion(f32[16,256,128]{2,1,0:T(8,128)S(1)} %fusion.66, f32[16,128,256]{2,1,0:T(8,128)S(1)} %fusion.91, f32[16,128,256]{2,1,0:T(8,128)S(1)} %fusion.82, f32[256,128]{0,1:T(8,128)S(1)} %get-tuple-element.17, f32[256,128]{0,1:T(8,128)S(1)} %get-tuple-element.18), kind=kOutput, calls=%fused_computation.65 | convolution fusion | flops 808157184 | bytes 8650752 | tf_op jit(solution)/shard_map/zcb,bd->zcd/dot_general | solution.py:26
  192.5 7.3 %multiply_subtract_fusion = (f32[16,256,128]{2,1,0:T(8,128)}, f32[16,256,128]{2,1,0:T(8,128)}, f32[16,256,128]{2,1,0:T(8,128)S(1)}, f32[16,256,128]{2,1,0:T(8,12...) fusion(f32[16,256,128]{2,1,0:T(8,128)S(1)} %copy-done.16, f32[16,256,128]{2,1,0:T(8,128)S(1)} %copy-done.18, ...), kind=kOutput, calls=%fused_computation.28 | convolution fusion | flops 817594368 | bytes 29622272 | tf_op jit(solution)/shard_map/zcb,bd->zcd/dot_general | solution.py:26
  199.8 2.3 fusion.145
  202.1 2.3 fusion.143
  204.3 2.3 convolution_subtract_fusion.3
  206.6 2.3 convolution_add_fusion.3
  208.9 3.0 fusion.22
  211.9 3.4 fusion.36
  219.9 2.3 fusion.137
  224.4 2.3 convolution_add_fusion.1
  226.7 3.2 fusion.14
  229.9 4.0 %fusion.39 = bf16[16,256,128]{1,2,0:T(8,128)(2,1)} fusion(f32[16,128,256]{2,1,0:T(8,128)S(1)} %fusion.14, f32[16,256,128]{1,2,0:T(8,128)S(1)} %convolution_add_fusion.1, f32[16,256,128]{1,2,0:T(8,128)S(1)} %convolution_subtract_fusion.1, f32[256,128]{0,1:T(8,128)S(1)} %get-tuple-element.17, f32[256,128]{0,1:T(8,128)S(1)} %get-tuple-element.18), kind=kOutput, calls=%fused_computation.68 | convolution fusion | flops 1614675968 | bytes 7602176 | tf_op jit(solution)/shard_map/ac,zcb->zab/dot_general | solution.py:47
  240.6 12.8 %all-to-all-start.6 = ((bf16[16,64,256]{2,0,1:T(8,128)(2,1)}), bf16[16,64,256]{2,0,1:T(8,128)(2,1)S(1)}, u32[]{:S(2)}, u32[]{:S(2)}) async-start(bf16[16,64,256]{2,0,1:T(8,128)(2,1)} %bitcast.274), calls=%async_computation.6 | async-start | bytes 1048576 | tf_op jit(solution)/shard_map/all_to_all | solution.py:118
  253.5 2.3 fusion.133
  255.8 3.6 fusion.135
  259.4 3.7 %convolution_add_fusion = f32[16,256,128]{1,2,0:T(8,128)} fusion(f32[16,256,128]{1,2,0:T(8,128)S(1)} %fusion.133, f32[16,256,128]{2,1,0:T(8,128)S(1)} %copy-done.3), kind=kOutput, calls=%fused_computation.55 | convolution fusion | flops 806060032 | bytes 6291456 | tf_op jit(solution)/shard_map/zcd,db->zcb/dot_general | solution.py:42
  263.1 7.9 %all-to-all-done.6 = bf16[16,64,256]{2,0,1:T(8,128)(2,1)S(1)} async-done(((bf16[16,64,256]{2,0,1:T(8,128)(2,1)}), bf16[16,64,256]{2,0,1:T(8,128)(2,1)S(1)}, u32[]{:S(2)}, u32[]{:S(2)}) %all-to-all-start.6) | async-done | bytes 524320 | tf_op jit(solution)/shard_map/all_to_all | solution.py:118
  270.9 5.7 %all-to-all-start.7 = ((bf16[16,64,256]{2,0,1:T(8,128)(2,1)}), bf16[16,64,256]{2,0,1:T(8,128)(2,1)}, u32[]{:S(2)}, u32[]{:S(2)}) async-start(bf16[16,64,256]{2,0,1:T(8,128)(2,1)} %bitcast.271), calls=%async_computation.7 | async-start | bytes 1048576 | tf_op jit(solution)/shard_map/all_to_all | solution.py:119
  276.6 4.1 %convolution_subtract_fusion = f32[16,256,128]{1,2,0:T(8,128)S(1)} fusion(f32[16,256,128]{1,2,0:T(8,128)} %fusion.135, f32[16,256,128]{2,1,0:T(8,128)S(1)} %copy-done.2), kind=kOutput, calls=%fused_computation.56 | convolution fusion | flops 806060032 | bytes 6291456 | tf_op jit(solution)/shard_map/zcd,db->zcb/dot_general | solution.py:39
  280.7 3.0 fusion.6
  283.7 4.4 %multiply_bitcast_fusion = f32[16,256,128]{1,2,0:T(8,128)} fusion(f32[16,128,256]{2,1,0:T(8,128)S(1)} %fusion.6, f32[16,256,128]{1,2,0:T(8,128)S(1)} %copy-done.6, f32[16,256,128]{1,2,0:T(8,128)S(1)} %convolution_subtract_fusion, f32[256,128]{0,1:T(8,128)S(1)} %get-tuple-element.17, f32[256,128]{0,1:T(8,128)S(1)} %get-tuple-element.18), kind=kOutput, calls=%fused_computation.19 | convolution fusion | flops 1614151680 | bytes 8650752 | tf_op jit(solution)/shard_map/ac,zcb->zab/dot_general | solution.py:47
  290.0 2.6 copy.208
  294.0 12.3 %all-to-all-start.4 = ((bf16[16,64,256]{2,0,1:T(8,128)(2,1)}), bf16[16,64,256]{2,0,1:T(8,128)(2,1)S(1)}, u32[]{:S(2)}, u32[]{:S(2)}) async-start(bf16[16,64,256]{2,0,1:T(8,128)(2,1)} %bitcast.273), calls=%async_computation.4 | async-start | bytes 1048576 | tf_op jit(solution)/shard_map/all_to_all | solution.py:117
  307.5 16.3 %all-to-all-done.4 = bf16[16,64,256]{2,0,1:T(8,128)(2,1)S(1)} async-done(((bf16[16,64,256]{2,0,1:T(8,128)(2,1)}), bf16[16,64,256]{2,0,1:T(8,128)(2,1)S(1)}, u32[]{:S(2)}, u32[]{:S(2)}) %all-to-all-start.4) | async-done | bytes 524320 | tf_op jit(solution)/shard_map/all_to_all | solution.py:117
  323.8 4.5 %all-to-all-start.8 = ((f32[16,64,256]{2,0,1:T(8,128)}), f32[16,64,256]{2,0,1:T(8,128)S(1)}, u32[]{:S(2)}, u32[]{:S(2)}) async-start(f32[16,64,256]{2,0,1:T(8,128)} %bitcast.241), calls=%async_computation.8 | async-start | bytes 2097152 | tf_op jit(solution)/shard_map/all_to_all | solution.py:121
  328.3 29.3 %all-to-all-done.8 = f32[16,64,256]{2,0,1:T(8,128)S(1)} async-done(((f32[16,64,256]{2,0,1:T(8,128)}), f32[16,64,256]{2,0,1:T(8,128)S(1)}, u32[]{:S(2)}, u32[]{:S(2)}) %all-to-all-start.8) | async-done | bytes 1048608 | tf_op jit(solution)/shard_map/all_to_all | solution.py:121
  (81 shorter events, 29.9 us)
Async XLA Ops:
  0.6 60.0 %copy-start.20 = (bf16[1024,256]{1,0:T(8,128)(2,1)S(1)}, bf16[1024,256]{1,0:T(8,128)(2,1)}, u32[]{:S(2)}) copy-start(bf16[1024,256]{1,0:T(8,128)(2,1)} %param.9) | copy-start | bytes 1572868
  83.1 22.7 %all-to-all-start.5 = ((bf16[64,16,256]{2,1,0:T(8,128)(2,1)}), bf16[64,16,256]{2,1,0:T(8,128)(2,1)S(1)}, u32[]{:S(2)}, u32[]{:S(2)}) async-start(bf16[64,16,256]{2,1,0:T(8,128)(2,1)} %bitcast.19), calls=%async_computation.5 | async-start | bytes 1048576 | tf_op jit(solution)/shard_map/all_to_all | solution.py:101
  89.1 22.7 %copy-start.9 = (f32[64,2,8,256]{3,2,0,1:T(8,128)}, f32[64,2,8,256]{3,2,0,1:T(8,128)S(1)}, u32[]{:S(2)}) copy-start(f32[64,2,8,256]{3,2,0,1:T(8,128)S(1)} %copy.190) | copy-start | bytes 3145732
  89.4 22.5 %copy-start.11 = (f32[64,2,8,256]{3,2,0,1:T(8,128)}, f32[64,2,8,256]{3,2,0,1:T(8,128)S(1)}, u32[]{:S(2)}) copy-start(f32[64,2,8,256]{3,2,0,1:T(8,128)S(1)} %copy.192) | copy-start | bytes 3145732
  105.8 59.6 %all-to-all-start.3 = ((f32[64,16,256]{2,1,0:T(8,128)}), f32[64,16,256]{2,1,0:T(8,128)}, u32[]{:S(2)}, u32[]{:S(2)}) async-start(f32[64,16,256]{2,1,0:T(8,128)} %bitcast.275), calls=%async_computation.3 | async-start | bytes 2097152 | tf_op jit(solution)/shard_map/all_to_all | solution.py:99
  111.6 1.2 copy-start.13
  113.1 17.5 %copy-start.7 = (f32[16,16384]{1,0:T(8,128)}, f32[16,16384]{1,0:T(8,128)S(1)}, u32[]{:S(2)}) copy-start(f32[16,16384]{1,0:T(8,128)S(1)} %get-tuple-element.20) | copy-start | bytes 3145732
  140.3 19.8 %copy-start = (f32[16,128,256]{2,1,0:T(8,128)}, f32[16,128,256]{2,1,0:T(8,128)S(1)}, u32[]{:S(2)}) copy-start(f32[16,128,256]{2,1,0:T(8,128)S(1)} %fusion.88) | copy-start | bytes 6291460
  184.6 7.9 %copy-start.18 = (f32[16,256,128]{2,1,0:T(8,128)S(1)}, f32[16,256,128]{2,1,0:T(8,128)}, u32[]{:S(2)}) copy-start(f32[16,256,128]{2,1,0:T(8,128)} %convolution_subtract_fusion.2) | copy-start | bytes 6291460
  188.5 4.0 %copy-start.1 = (f32[16,128,256]{2,1,0:T(8,128)S(1)}, f32[16,128,256]{2,1,0:T(8,128)}, u32[]{:S(2)}) copy-start(f32[16,128,256]{2,1,0:T(8,128)} %copy-done) | copy-start | bytes 6291460
  188.5 4.0 %copy-start.15 = (f32[16,256,128]{2,1,0:T(8,128)S(1)}, f32[16,256,128]{2,1,0:T(8,128)}, u32[]{:S(2)}) copy-start(f32[16,256,128]{2,1,0:T(8,128)} %fusion.72) | copy-start | bytes 6291460
  188.5 4.0 %copy-start.16 = (f32[16,256,128]{2,1,0:T(8,128)S(1)}, f32[16,256,128]{2,1,0:T(8,128)}, u32[]{:S(2)}) copy-start(f32[16,256,128]{2,1,0:T(8,128)} %convolution_subtract_fusion.5) | copy-start | bytes 6291460
  188.5 4.0 %copy-start.17 = (f32[16,256,128]{2,1,0:T(8,128)S(1)}, f32[16,256,128]{2,1,0:T(8,128)}, u32[]{:S(2)}) copy-start(f32[16,256,128]{2,1,0:T(8,128)} %convolution_add_fusion.5) | copy-start | bytes 6291460
  216.0 1.6 copy-start.4
  217.6 2.3 copy-start.5
  233.9 2.5 copy-start.14
  235.6 1.2 copy-start.8
  235.6 1.5 copy-start.10
  235.6 1.8 copy-start.12
  238.9 14.5 %copy-start.2 = (f32[16,256,128]{2,1,0:T(8,128)S(1)}, f32[16,256,128]{2,1,0:T(8,128)}, u32[]{:S(2)}) copy-start(f32[16,256,128]{2,1,0:T(8,128)} %get-tuple-element.4) | copy-start | bytes 6291460
  240.6 30.3 %all-to-all-start.6 = ((bf16[16,64,256]{2,0,1:T(8,128)(2,1)}), bf16[16,64,256]{2,0,1:T(8,128)(2,1)S(1)}, u32[]{:S(2)}, u32[]{:S(2)}) async-start(bf16[16,64,256]{2,0,1:T(8,128)(2,1)} %bitcast.274), calls=%async_computation.6 | async-start | bytes 1048576 | tf_op jit(solution)/shard_map/all_to_all | solution.py:118
  253.5 2.3 copy-start.3
  270.9 23.0 %all-to-all-start.7 = ((bf16[16,64,256]{2,0,1:T(8,128)(2,1)}), bf16[16,64,256]{2,0,1:T(8,128)(2,1)}, u32[]{:S(2)}, u32[]{:S(2)}) async-start(bf16[16,64,256]{2,0,1:T(8,128)(2,1)} %bitcast.271), calls=%async_computation.7 | async-start | bytes 1048576 | tf_op jit(solution)/shard_map/all_to_all | solution.py:119
  276.6 4.1 %copy-start.6 = (f32[16,256,128]{1,2,0:T(8,128)S(1)}, f32[16,256,128]{1,2,0:T(8,128)}, u32[]{:S(2)}) copy-start(f32[16,256,128]{1,2,0:T(8,128)} %convolution_add_fusion) | copy-start | bytes 6291460
  292.6 13.7 %copy-start.19 = (f32[2,8,256,128]{3,1,2,0:T(8,128)S(1)}, f32[2,8,256,128]{3,1,2,0:T(8,128)}, u32[]{:S(2)}) copy-start(f32[2,8,256,128]{3,1,2,0:T(8,128)} %copy.208) | copy-start | bytes 6291460
  294.0 29.8 %all-to-all-start.4 = ((bf16[16,64,256]{2,0,1:T(8,128)(2,1)}), bf16[16,64,256]{2,0,1:T(8,128)(2,1)S(1)}, u32[]{:S(2)}, u32[]{:S(2)}) async-start(bf16[16,64,256]{2,0,1:T(8,128)(2,1)} %bitcast.273), calls=%async_computation.4 | async-start | bytes 1048576 | tf_op jit(solution)/shard_map/all_to_all | solution.py:117
  323.8 33.8 %all-to-all-start.8 = ((f32[16,64,256]{2,0,1:T(8,128)}), f32[16,64,256]{2,0,1:T(8,128)S(1)}, u32[]{:S(2)}, u32[]{:S(2)}) async-start(f32[16,64,256]{2,0,1:T(8,128)} %bitcast.241), calls=%async_computation.8 | async-start | bytes 2097152 | tf_op jit(solution)/shard_map/all_to_all | solution.py:121
where the time goes:
time: 368 us; the launch traced here: 362 us
  matrix products  136 us (37%)
  blocking collectives  82.4 us (22%)
  waiting for transfers between devices  69.1 us (19%)
  starting transfers between devices  45.6 us (12%)
  local copies, waits for them, and re-layouts  24.5 us (7%)
    all_to_all x1, blocking collectives, local(): lax.all_to_all(k_field, 'ctx', split_axis=0, concat_axis=1, tiled=True)  36.3 us
    all_to_all x1, waiting for transfers between devices, local(): lax.all_to_all(taps_grad, 'ctx', split_axis=1, concat_axis=0, tiled=True)  29.3 us
    all_to_all x1, blocking collectives, local(): lax.all_to_all(v_field, 'ctx', split_axis=0, concat_axis=1, tiled=True)  23.7 us
    all_to_all x1, blocking collectives, local(): lax.all_to_all(out_grad, 'ctx', split_axis=0, concat_axis=1, tiled=True)  22.4 us
    dot_general x3, matrix products, forward_transform(): jnp.einsum('zcb,bd->zcd', turned_imag, sine_cols, precision=highest)  16.4 us
    all_to_all x1, waiting for transfers between devices, local(): lax.all_to_all(grads_chan[0], 'ctx', split_axis=1, concat_axis=0, tiled=T...  16.3 us
    all_to_all x1, waiting for transfers between devices, local(): lax.all_to_all(q_field, 'ctx', split_axis=0, concat_axis=1, tiled=True)  15 us
    dot_general x3, matrix products, forward_transform(): jnp.einsum('zcb,bd->zcd', turned_real, sine_cols, precision=highest)  14.7 us
  transfers between devices with their start and end apart: 6, of which 5 were waited for; matrix products, arithmetic and copies ran while one was open for 23% of the time, Pallas kernels for 0%

commit v1 on v0

v1 whole, which is shorter than its diff:
```python
import functools

import jax
import jax.numpy as jnp
import ml_dtypes
import numpy as np
from jax import lax
from jax.experimental import pallas as pl
from jax.experimental.pallas import tpu as pltpu
from jax.sharding import PartitionSpec as P

MESH = pl.DeviceIdType.MESH
BF16 = jnp.bfloat16
F32 = jnp.float32


def split_table(table, axis):
    high = table.astype(ml_dtypes.bfloat16)
    low = (table - high.astype(np.float64)).astype(ml_dtypes.bfloat16)
    return np.concatenate([high, low], axis=axis)


def make_tables(blocks, width):
    a = np.arange(blocks)[:, None]
    c = np.arange(blocks)[None, :] + 0.5
    phase = 2 * np.pi * a * c / (2 * blocks)
    first = split_table(np.concatenate([np.cos(phase).T, -np.sin(phase).T], axis=0), 1)
    last = split_table(np.concatenate([np.cos(phase), -np.sin(phase)], axis=1), 1)
    b = np.arange(width)
    turn = 2 * np.pi * c.T * b[None, :] / (2 * blocks * width)
    twist = np.concatenate([np.cos(turn), np.sin(turn)], axis=0).astype(np.float32)
    angle = 2 * np.pi * ((b[:, None] * b[None, :]) % width) / width
    cos, sin = np.cos(angle), np.sin(angle)
    forth = np.block([[cos, -sin], [sin, cos]]).astype(ml_dtypes.bfloat16)
    back = np.block([[cos, sin], [-sin, cos]]).astype(ml_dtypes.bfloat16)
    return first, last, twist, forth, back


def dot(x, y):
    return jnp.dot(x, y, preferred_element_type=F32)


def kernel(
    blocks, count, width,
    k_hbm, v_hbm, g_hbm, q_hbm, taps_hbm, first_hbm, last_hbm, twist_hbm, forth_hbm, back_hbm,
    fwd_out, bwd_out, tap_out,
    k_in, v_in, g_in, q_in, taps_in, first, last, twist, forth, back,
    sent, arrived, packed, wide, gated_spec, taps_spec, prod_spec, mixed,
    load_sem, own_sem, send_sem, recv_sem,
):
    me = lax.axis_index("ctx")
    rows = blocks * count
    lanes = 128
    halves = width // lanes
    loads = [
        pltpu.make_async_copy(src, dst, load_sem.at[i])
        for i, (src, dst) in enumerate(
            (
                (k_hbm, k_in), (v_hbm, v_in), (taps_hbm, taps_in), (g_hbm, g_in), (q_hbm, q_in),
                (first_hbm, first), (last_hbm, last), (twist_hbm, twist), (forth_hbm, forth), (back_hbm, back),
            )
        )
    ]
    for load in loads:
        load.start()

    barrier = pltpu.get_barrier_semaphore()

    def greet(j, carry):
        peer = lax.rem(me + j, blocks)
        pl.semaphore_signal(barrier, inc=1, device_id={"ctx": peer}, device_id_type=MESH)
        return carry

    lax.fori_loop(1, blocks, greet, 0)

    def own_rows():
        return pl.ds(pl.multiple_of(me * count, count), count)

    def send(i, target):
        def one(j, carry):
            peer = lax.rem(me + j, blocks)
            pltpu.make_async_remote_copy(
                src_ref=sent.at[i, pl.ds(pl.multiple_of(peer * count, count), count)],
                dst_ref=target.at[own_rows()],
                send_sem=send_sem.at[i],
                recv_sem=recv_sem.at[i],
                device_id={"ctx": peer},
                device_id_type=MESH,
            ).start()
            return carry

        lax.fori_loop(1, blocks, one, 0)

    def wait_all(i, target, sem):
        part = pl.ds(0, rows - count)
        pltpu.make_async_copy(target.at[part], target.at[part], sem.at[i]).wait()

    loads[0].wait()
    loads[1].wait()
    sent[0] = (k_in[...].astype(F32) * v_in[...].astype(F32)).astype(BF16)
    pl.semaphore_wait(barrier, blocks - 1)
    send(0, arrived.at[0])
    loads[2].wait()
    sent[1] = taps_in[...].astype(BF16)
    send(1, arrived.at[1])
    loads[3].wait()
    loads[4].wait()
    sent[2] = (g_in[...].astype(F32) * q_in[...].astype(F32)).astype(BF16)
    send(2, arrived.at[2])
    for load in loads[5:]:
        load.wait()

    group = 4
    tile = group * blocks

    def transform(i, spec):
        wait_all(i, arrived.at[i], recv_sem)
        arrived[i, own_rows()] = sent[i, own_rows()]
        for h in range(halves):
            wide[h] = arrived[i, :, lanes * h : lanes * (h + 1)].astype(F32)

        def one(t, carry):
            for s in range(group):
                every = pl.ds(t * group + s, blocks, stride=count)
                x = jnp.concatenate([wide[h, every, :] for h in range(halves)], axis=1).astype(BF16)
                y = dot(first[...], jnp.concatenate([x, x], axis=0))
                real, imag = y[:blocks], y[blocks:]
                cos, sin = twist[:blocks], twist[blocks:]
                packed[s * blocks : (s + 1) * blocks, :width] = (real * cos + imag * sin).astype(BF16)
                packed[s * blocks : (s + 1) * blocks, width:] = (imag * cos - real * sin).astype(BF16)
            spec[pl.ds(pl.multiple_of(t * tile, tile), tile), :] = dot(packed[...], forth[...])
            return carry

        lax.fori_loop(0, count // group, one, 0)

    def multiply_back(i, left, right, conjugate, scale):
        def one(t, carry):
            part = pl.ds(pl.multiple_of(t * tile, tile), tile)
            lr, li = left[part, :width], left[part, width:]
            rr, ri = right[part, :width], right[part, width:]
            if conjugate:
                mixed[:, :width] = (lr * rr + li * ri).astype(BF16)
                mixed[:, width:] = (li * rr - lr * ri).astype(BF16)
            else:
                mixed[:, :width] = (lr * rr - li * ri).astype(BF16)
                mixed[:, width:] = (lr * ri + li * rr).astype(BF16)
            u = dot(mixed[...], back[...])
            cos, sin = twist[:blocks] * scale, twist[blocks:] * scale
            for s in range(group):
                real = u[s * blocks : (s + 1) * blocks, :width]
                imag = u[s * blocks : (s + 1) * blocks, width:]
                turned = jnp.concatenate(
                    [(real * cos - imag * sin).astype(BF16), (imag * cos + real * sin).astype(BF16)], axis=0
                )
                out = dot(last[...], jnp.concatenate([turned, turned], axis=0))
                for h in range(halves):
                    wide[h, pl.ds(t * group + s, blocks, stride=count), :] = out[:, lanes * h : lanes * (h + 1)]
            return carry

        lax.fori_loop(0, count // group, one, 0)
        for h in range(halves):
            sent[i, :, lanes * h : lanes * (h + 1)] = wide[h].astype(BF16)

    def give(i, out):
        own = pltpu.make_async_copy(sent.at[i, own_rows()], out.at[own_rows()], own_sem.at[i - 3])
        send(i, out)
        own.start()
        return own

    norm = 1.0 / (blocks * width)
    transform(0, gated_spec)
    transform(1, taps_spec)
    multiply_back(3, gated_spec, taps_spec, False, norm)
    owns = [give(3, fwd_out)]
    transform(2, prod_spec)
    multiply_back(4, prod_spec, taps_spec, True, norm)
    owns.append(give(4, bwd_out))
    multiply_back(5, prod_spec, gated_spec, True, norm * (blocks * width) ** -0.5)
    owns.append(give(5, tap_out))
    for own in owns:
        own.wait()
    for i in range(6):
        wait_all(i, sent.at[i], send_sem)
    for i, out in ((3, fwd_out), (4, bwd_out), (5, tap_out)):
        wait_all(i, out, recv_sem)


def exchange_convolve(k_field, v_field, out_grad, q_field, taps, blocks):
    channels, width = k_field.shape
    count = channels // blocks
    rows = channels
    tables = make_tables(blocks, width)
    any_space = pl.BlockSpec(memory_space=pl.ANY)
    field = pltpu.VMEM((rows, width), BF16)
    spectrum = pltpu.VMEM((rows, 2 * width), F32)
    table_space = [pltpu.VMEM(t.shape, t.dtype) for t in tables]
    dma = pltpu.SemaphoreType.DMA
    return pl.pallas_call(
        functools.partial(kernel, blocks, count, width),
        out_shape=[jax.ShapeDtypeStruct((rows, width), BF16)] * 3,
        in_specs=[any_space] * 10,
        out_specs=[any_space] * 3,
        scratch_shapes=[
            field, field, field, field, pltpu.VMEM((rows, width), F32), *table_space,
            pltpu.VMEM((6, rows, width), BF16),
            pltpu.VMEM((3, rows, width), BF16),
            pltpu.VMEM((4 * blocks, 2 * width), BF16),
            pltpu.VMEM((width // 128, rows, 128), F32),
            spectrum, spectrum, spectrum,
            pltpu.VMEM((4 * blocks, 2 * width), BF16),
            dma((10,)), dma((3,)), dma((6,)), dma((6,)),
        ],
        compiler_params=pltpu.CompilerParams(
            collective_id=0, has_side_effects=True, vmem_limit_bytes=48 * 2**20
        ),
        name="exchange_convolve",
    )(k_field, v_field, out_grad, q_field, taps, *[jnp.asarray(t) for t in tables])


def local(blocks, q_field, k_field, v_field, out_grad, filter_taps, skip):
    fwd, bwd, tap = exchange_convolve(k_field, v_field, out_grad, q_field, filter_taps, blocks)
    wide = lambda x: x.astype(F32)
    skip_col = skip[:, None]
    gated = wide((wide(k_field) * wide(v_field)).astype(BF16))
    product = wide((wide(out_grad) * wide(q_field)).astype(BF16))
    q_grad = (wide(out_grad) * (wide(fwd) + skip_col * gated)).astype(BF16)
    z_grad = wide(bwd) + skip_col * product
    k_grad = (wide(v_field) * z_grad).astype(BF16)
    v_grad = (wide(k_field) * z_grad).astype(BF16)
    return q_grad, k_grad, v_grad, wide(tap)


def solution(mesh):
    spec = P("tp", "ctx")
    return jax.shard_map(
        functools.partial(local, mesh.shape["ctx"]),
        mesh=mesh,
        in_specs=(spec, spec, spec, spec, spec, P("tp")),
        out_specs=(spec, spec, spec, spec),
        check_vma=False,
    )
```

time: 368 us -> 99.4 us (0.27)
  the two profiles are of different devices: /device:TPU:33 before, /device:TPU:65 now
where the time goes in v1:
time: 99.4 us; the launch traced here: 98.8 us
  Pallas kernels  84.8 us (85%)
  local copies, waits for them, and re-layouts  10.6 us (11%)
  other arithmetic  2.81 us (3%)
    pallas_call x1, Pallas kernels, exchange_convolve(): pl.pallas_call(functools.partial(kernel, blocks, count, width), out_shape...  84.8 us
    unnamed x22, local copies, waits for them, and re-layouts  10.6 us

profile of v1, /device:TPU:65, one launch (start us, length us, event | category | flops | bytes accessed | tf_op | source)
XLA Modules:
  0.0 98.8 jit_solution(3234070574651729662)
XLA Ops:
  0.6 0.0 copy-start
  0.6 1.0 %copy-done = bf16[1024,256]{1,0:T(8,128)(2,1)S(1)} copy-done((bf16[1024,256]{1,0:T(8,128)(2,1)S(1)}, bf16[1024,256]{1,0:T(8,128)(2,1)}, u32[]{:S(2)}) %copy-start) | copy-done | bytes 524312
  1.7 0.0 copy-start.1
  1.7 1.0 %copy-done.1 = bf16[1024,256]{1,0:T(8,128)(2,1)S(1)} copy-done((bf16[1024,256]{1,0:T(8,128)(2,1)S(1)}, bf16[1024,256]{1,0:T(8,128)(2,1)}, u32[]{:S(2)}) %copy-start.1) | copy-done | bytes 524312
  2.7 0.0 copy-start.2
  2.7 1.0 %copy-done.2 = bf16[1024,256]{1,0:T(8,128)(2,1)S(1)} copy-done((bf16[1024,256]{1,0:T(8,128)(2,1)S(1)}, bf16[1024,256]{1,0:T(8,128)(2,1)}, u32[]{:S(2)}) %copy-start.2) | copy-done | bytes 524312
  3.8 0.0 copy-start.3
  3.8 1.0 %copy-done.3 = bf16[1024,256]{1,0:T(8,128)(2,1)S(1)} copy-done((bf16[1024,256]{1,0:T(8,128)(2,1)S(1)}, bf16[1024,256]{1,0:T(8,128)(2,1)}, u32[]{:S(2)}) %copy-start.3) | copy-done | bytes 524312
  4.8 0.0 copy-start.4
  4.8 1.2 %copy-done.4 = f32[1024,256]{1,0:T(8,128)S(1)} copy-done((f32[1024,256]{1,0:T(8,128)S(1)}, f32[1024,256]{1,0:T(8,128)}, u32[]{:S(2)}) %copy-start.4) | copy-done | bytes 1048600
  6.0 0.0 copy-start.5
  6.0 1.0 %copy-done.5 = bf16[512,512]{1,0:T(8,128)(2,1)S(1)} copy-done((bf16[512,512]{1,0:T(8,128)(2,1)S(1)}, bf16[512,512]{1,0:T(8,128)(2,1)}, u32[]{:S(2)}) %copy-start.5) | copy-done | bytes 524312
  7.1 0.0 copy-start.6
  7.1 1.0 %copy-done.6 = bf16[512,512]{1,0:T(8,128)(2,1)S(1)} copy-done((bf16[512,512]{1,0:T(8,128)(2,1)S(1)}, bf16[512,512]{1,0:T(8,128)(2,1)}, u32[]{:S(2)}) %copy-start.6) | copy-done | bytes 524312
  8.1 0.0 copy-start.7
  8.1 0.9 copy-done.7
  9.0 0.0 copy-start.8
  9.0 0.8 copy-done.8
  9.8 0.0 copy-start.9
  9.8 0.8 copy-done.9
  10.5 84.8 %exchange_convolve.1 = (bf16[1024,256]{1,0:T(8,128)(2,1)S(1)}, bf16[1024,256]{1,0:T(8,128)(2,1)S(1)}, bf16[1024,256]{1,0:T(8,128)(2,1)S(1)}) custom-call(bf16[1024,256]{1,0:T(8,128)(2,1)S(1)} %copy-done, bf16[1024,256]{1,0:T(8,128)(2,1)S(1)} %copy-done.1, bf16[1024,256]{1,0:T(8,128)(2,1)S(1)} %copy-done.2, bf16[1024,256]{1,0:T(8,128)(2,1)S(1)} %copy-done.3, ...), custom_call_target="tpu_custom_call" | custom-call | tf_op jit(solution)/shard_map/exchange_convolve/pallas_call | solution.py:198
  95.3 0.0 copy-start.10
  95.3 0.7 copy-done.10
  96.0 1.8 %fusion.2 = (bf16[1024,256]{1,0:T(8,128)(2,1)}, bf16[1024,256]{1,0:T(8,128)(2,1)}, bf16[1024,256]{1,0:T(8,128)(2,1)}) fusion(bf16[1024,256]{1,0:T(8,128)(2,1)S(1)} %copy-done, bf16[1024,256]{1,0:T(8,128)(2,1)S(1)} %get-tuple-element.8, f32[1024]{0:T(1024)S(1)} %copy-done.10, bf16[1024,256]{1,0:T(8,128)(2,1)S(1)} %copy-done.3, ...), kind=kLoop, calls=%fused_computation.7 | loop fusion | flops 5767168 | bytes 4722688 | tf_op jit(solution)/shard_map/convert_element_type | solution.py:229
  97.8 1.0 %convert_element_type.58 = f32[1024,256]{1,0:T(8,128)} convert(bf16[1024,256]{1,0:T(8,128)(2,1)S(1)} %get-tuple-element.9) | non-fusion elementwise | flops 262144 | bytes 1572864 | tf_op jit(solution)/shard_map/convert_element_type | solution.py:222
Async XLA Ops:
  0.6 1.0 %copy-start = (bf16[1024,256]{1,0:T(8,128)(2,1)S(1)}, bf16[1024,256]{1,0:T(8,128)(2,1)}, u32[]{:S(2)}) copy-start(bf16[1024,256]{1,0:T(8,128)(2,1)} %k_hbm.1) | copy-start | bytes 1572868
  1.7 1.0 %copy-start.1 = (bf16[1024,256]{1,0:T(8,128)(2,1)S(1)}, bf16[1024,256]{1,0:T(8,128)(2,1)}, u32[]{:S(2)}) copy-start(bf16[1024,256]{1,0:T(8,128)(2,1)} %v_hbm.1) | copy-start | bytes 1572868
  2.7 1.0 %copy-start.2 = (bf16[1024,256]{1,0:T(8,128)(2,1)S(1)}, bf16[1024,256]{1,0:T(8,128)(2,1)}, u32[]{:S(2)}) copy-start(bf16[1024,256]{1,0:T(8,128)(2,1)} %g_hbm.1) | copy-start | bytes 1572868
  3.8 1.0 %copy-start.3 = (bf16[1024,256]{1,0:T(8,128)(2,1)S(1)}, bf16[1024,256]{1,0:T(8,128)(2,1)}, u32[]{:S(2)}) copy-start(bf16[1024,256]{1,0:T(8,128)(2,1)} %q_hbm.1) | copy-start | bytes 1572868
  4.8 1.2 %copy-start.4 = (f32[1024,256]{1,0:T(8,128)S(1)}, f32[1024,256]{1,0:T(8,128)}, u32[]{:S(2)}) copy-start(f32[1024,256]{1,0:T(8,128)} %taps_hbm.1) | copy-start | bytes 3145732
  6.0 1.0 %copy-start.5 = (bf16[512,512]{1,0:T(8,128)(2,1)S(1)}, bf16[512,512]{1,0:T(8,128)(2,1)}, u32[]{:S(2)}) copy-start(bf16[512,512]{1,0:T(8,128)(2,1)} %constant.14.clone.back_hbm) | copy-start | bytes 1572868
  7.1 1.0 %copy-start.6 = (bf16[512,512]{1,0:T(8,128)(2,1)S(1)}, bf16[512,512]{1,0:T(8,128)(2,1)}, u32[]{:S(2)}) copy-start(bf16[512,512]{1,0:T(8,128)(2,1)} %constant.13.clone.forth_hbm) | copy-start | bytes 1572868
  8.1 0.9 copy-start.7
  9.0 0.8 copy-start.8
  9.8 0.8 copy-start.9
  95.3 0.7 copy-start.10

commit v2 on v1

--- a/solution.py
+++ b/solution.py
@@ -42,11 +42,11 @@
 
 def kernel(
     blocks, count, width,
-    k_hbm, v_hbm, g_hbm, q_hbm, taps_hbm, first_hbm, last_hbm, twist_hbm, forth_hbm, back_hbm,
-    fwd_out, bwd_out, tap_out,
-    k_in, v_in, g_in, q_in, taps_in, first, last, twist, forth, back,
-    sent, arrived, packed, wide, gated_spec, taps_spec, prod_spec, mixed,
-    load_sem, own_sem, send_sem, recv_sem,
+    k_hbm, v_hbm, g_hbm, q_hbm, taps_hbm, skip_hbm, first_hbm, last_hbm, twist_hbm, forth_hbm, back_hbm,
+    q_hbm_out, k_hbm_out, v_hbm_out, tap_out,
+    q_out, k_out, v_out, k_in, v_in, g_in, q_in, taps_in, skip_in, first, last, twist, forth, back,
+    sent, arrived, returned, packed, wide, gated_spec, taps_spec, prod_spec, mixed,
+    load_sem, store_sem, own_sem, send_sem, recv_sem,
 ):
     me = lax.axis_index("ctx")
     rows = blocks * count
@@ -57,7 +57,7 @@
         for i, (src, dst) in enumerate(
             (
                 (k_hbm, k_in), (v_hbm, v_in), (taps_hbm, taps_in), (g_hbm, g_in), (q_hbm, q_in),
-                (first_hbm, first), (last_hbm, last), (twist_hbm, twist), (forth_hbm, forth), (back_hbm, back),
+                (skip_hbm, skip_in), (first_hbm, first), (last_hbm, last), (twist_hbm, twist), (forth_hbm, forth), (back_hbm, back),
             )
         )
     ]
@@ -161,73 +161,129 @@
         for h in range(halves):
             sent[i, :, lanes * h : lanes * (h + 1)] = wide[h].astype(BF16)
 
-    def give(i, out):
-        own = pltpu.make_async_copy(sent.at[i, own_rows()], out.at[own_rows()], own_sem.at[i - 3])
-        send(i, out)
-        own.start()
-        return own
+    def give(i, target):
+        send(i, target)
+        target[own_rows()] = sent[i, own_rows()]
 
     norm = 1.0 / (blocks * width)
+    fwd, bwd = returned.at[0], returned.at[1]
     transform(0, gated_spec)
     transform(1, taps_spec)
     multiply_back(3, gated_spec, taps_spec, False, norm)
-    owns = [give(3, fwd_out)]
+    give(3, fwd)
     transform(2, prod_spec)
     multiply_back(4, prod_spec, taps_spec, True, norm)
-    owns.append(give(4, bwd_out))
+    give(4, bwd)
     multiply_back(5, prod_spec, gated_spec, True, norm * (blocks * width) ** -0.5)
-    owns.append(give(5, tap_out))
-    for own in owns:
-        own.wait()
+    own_taps = pltpu.make_async_copy(sent.at[5, own_rows()], tap_out.at[own_rows()], own_sem)
+    own_taps.start()
+    send(5, tap_out)
+
+    skip_cols = skip_in[...].T
+
+    def each_part(body):
+        for s in range(rows // lanes):
+            body(pl.ds(s * lanes, lanes), skip_cols[:, s : s + 1])
+
+    def finish_q(part, skip):
+        total = returned[0, part].astype(F32) + skip * sent[0, part].astype(F32)
+        q_out[part] = (g_in[part].astype(F32) * total).astype(BF16)
+
+    def finish_kv(part, skip):
+        z_grad = returned[1, part].astype(F32) + skip * sent[2, part].astype(F32)
+        k_out[part] = (v_in[part].astype(F32) * z_grad).astype(BF16)
+        v_out[part] = (k_in[part].astype(F32) * z_grad).astype(BF16)
+
+    stores = [
+        pltpu.make_async_copy(src, dst, store_sem.at[i])
+        for i, (src, dst) in enumerate(((q_out, q_hbm_out), (k_out, k_hbm_out), (v_out, v_hbm_out)))
+    ]
+    wait_all(3, fwd, recv_sem)
+    each_part(finish_q)
+    stores[0].start()
+    wait_all(4, bwd, recv_sem)
+    each_part(finish_kv)
+    stores[1].start()
+    stores[2].start()
+    own_taps.wait()
+    for store in stores:
+        store.wait()
     for i in range(6):
         wait_all(i, sent.at[i], send_sem)
-    for i, out in ((3, fwd_out), (4, bwd_out), (5, tap_out)):
-        wait_all(i, out, recv_sem)
-
-
-def exchange_convolve(k_field, v_field, out_grad, q_field, taps, blocks):
+    wait_all(5, tap_out, recv_sem)
+
+
+def store_kernel(q_ref, k_ref, v_ref, tap_ref, q_out, k_out, v_out, tap_out, held, wide, sems):
+    parts = 2
+    step = wide.shape[0] // parts
+    moves = []
+    for i, (src, dst) in enumerate(((tap_ref, tap_out), (q_ref, q_out), (k_ref, k_out), (v_ref, v_out))):
+        for p in range(parts):
+            rows = pl.ds(p * step, step)
+            stage = wide.at[rows] if i == 0 else held.at[i, rows]
+            load = pltpu.make_async_copy(src.at[rows], held.at[i, rows], sems.at[0, i, p])
+            store = pltpu.make_async_copy(stage, dst.at[rows], sems.at[1, i, p])
+            load.start()
+            moves.append((load, store, i, rows))
+    for load, store, i, rows in moves:
+        load.wait()
+        if i == 0:
+            wide[rows] = held[0, rows].astype(F32)
+        store.start()
+    for _, store, _, _ in moves:
+        store.wait()
+
+
+def exchange_convolve(k_field, v_field, out_grad, q_field, taps, skip, blocks):
     channels, width = k_field.shape
     count = channels // blocks
     rows = channels
+    lanes = 128
     tables = make_tables(blocks, width)
-    any_space = pl.BlockSpec(memory_space=pl.ANY)
+    hbm = pl.BlockSpec(memory_space=pltpu.HBM)
     field = pltpu.VMEM((rows, width), BF16)
     spectrum = pltpu.VMEM((rows, 2 * width), F32)
     table_space = [pltpu.VMEM(t.shape, t.dtype) for t in tables]
     dma = pltpu.SemaphoreType.DMA
-    return pl.pallas_call(
+    result = jax.ShapeDtypeStruct((rows, width), BF16)
+    grads = pl.pallas_call(
         functools.partial(kernel, blocks, count, width),
-        out_shape=[jax.ShapeDtypeStruct((rows, width), BF16)] * 3,
-        in_specs=[any_space] * 10,
-        out_specs=[any_space] * 3,
+        out_shape=[result] * 4,
+        in_specs=[hbm] * 11,
+        out_specs=[hbm] * 4,
         scratch_shapes=[
-            field, field, field, field, pltpu.VMEM((rows, width), F32), *table_space,
+            field, field, field, field, field, field, field,
+            pltpu.VMEM((rows, width), F32), pltpu.VMEM((rows // lanes, lanes), F32), *table_space,
             pltpu.VMEM((6, rows, width), BF16),
             pltpu.VMEM((3, rows, width), BF16),
+            pltpu.VMEM((2, rows, width), BF16),
             pltpu.VMEM((4 * blocks, 2 * width), BF16),
-            pltpu.VMEM((width // 128, rows, 128), F32),
+            pltpu.VMEM((width // lanes, rows, lanes), F32),
             spectrum, spectrum, spectrum,
             pltpu.VMEM((4 * blocks, 2 * width), BF16),
-            dma((10,)), dma((3,)), dma((6,)), dma((6,)),
+            dma((11,)), dma((3,)), dma, dma((6,)), dma((6,)),
         ],
         compiler_params=pltpu.CompilerParams(
-            collective_id=0, has_side_effects=True, vmem_limit_bytes=48 * 2**20
+            collective_id=0, has_side_effects=True, vmem_limit_bytes=58 * 2**20
         ),
         name="exchange_convolve",
-    )(k_field, v_field, out_grad, q_field, taps, *[jnp.asarray(t) for t in tables])
+    )(
+        k_field, v_field, out_grad, q_field, taps, skip.reshape(rows // lanes, lanes),
+        *[jnp.asarray(t) for t in tables],
+    )
+    return pl.pallas_call(
+        store_kernel,
+        out_shape=[result] * 3 + [jax.ShapeDtypeStruct((rows, width), F32)],
+        in_specs=[hbm] * 4,
+        out_specs=[hbm] * 4,
+        scratch_shapes=[pltpu.VMEM((4, rows, width), BF16), pltpu.VMEM((rows, width), F32), dma((2, 4, 2))],
+        compiler_params=pltpu.CompilerParams(vmem_limit_bytes=58 * 2**20),
+        name="store_grads",
+    )(*grads)
 
 
 def local(blocks, q_field, k_field, v_field, out_grad, filter_taps, skip):
-    fwd, bwd, tap = exchange_convolve(k_field, v_field, out_grad, q_field, filter_taps, blocks)
-    wide = lambda x: x.astype(F32)
-    skip_col = skip[:, None]
-    gated = wide((wide(k_field) * wide(v_field)).astype(BF16))
-    product = wide((wide(out_grad) * wide(q_field)).astype(BF16))
-    q_grad = (wide(out_grad) * (wide(fwd) + skip_col * gated)).astype(BF16)
-    z_grad = wide(bwd) + skip_col * product
-    k_grad = (wide(v_field) * z_grad).astype(BF16)
-    v_grad = (wide(k_field) * z_grad).astype(BF16)
-    return q_grad, k_grad, v_grad, wide(tap)
+    return tuple(exchange_convolve(k_field, v_field, out_grad, q_field, filter_taps, skip, blocks))
 
 
 def solution(mesh):

time: 99.4 us -> 87.9 us (0.88)
  local copies, waits for them, and re-layouts: 10.6 us -> 0 us
  other arithmetic: 2.81 us -> 0 us
  Pallas kernels: 84.8 us -> 87.1 us
    unnamed x22 -> x0, local copies, waits for them, and re-layouts: 10.6 us -> none
    convert_element_type x2 -> x0, other arithmetic: 2.81 us -> none  [the longest x1 1.77 us: local(): v_grad = (wide(k_field) * z_grad).astype(BF16)]
    pallas_call x0 -> x1, Pallas kernels: none -> 2.6 us  [exchange_convolve(): pl.pallas_call(store_kernel, out_shape=[result] * 3 + [jax.ShapeDtypeStru...]
where the time goes in v2:
time: 87.9 us; the launch traced here: 87.8 us
  Pallas kernels  87.1 us (99%)
    pallas_call x1, Pallas kernels, exchange_convolve(): pl.pallas_call(functools.partial(kernel, blocks, count, width), out_shape...  84.5 us
    pallas_call x1, Pallas kernels, exchange_convolve(): pl.pallas_call(store_kernel, out_shape=[result] * 3 + [jax.ShapeDtypeStru...  2.6 us

profile of v2, /device:TPU:65, one launch (start us, length us, event | category | flops | bytes accessed | tf_op | source)
XLA Modules:
  0.0 87.8 jit_solution(16214259396982938805)
XLA Ops:
  0.6 84.5 %exchange_convolve.1 = (bf16[1024,256]{1,0:T(8,128)(2,1)}, bf16[1024,256]{1,0:T(8,128)(2,1)}, bf16[1024,256]{1,0:T(8,128)(2,1)}, bf16[1024,256]{1,0:T(8,128)(2,1)}) custom-call(bf16[1024,256]{1,0:T(8,128)(2,1)} %k_hbm.1, bf16[1024,256]{1,0:T(8,128)(2,1)} %v_hbm.1, bf16[1024,256]{1,0:T(8,128)(2,1)} %g_hbm.1, bf16[1024,256]{1,0:T(8,128)(2,1)} %q_hbm.1, ...), custom_call_target="tpu_custom_call" | custom-call | tf_op jit(solution)/shard_map/exchange_convolve/pallas_call | solution.py:249
  85.2 2.6 %store_grads.1 = (bf16[1024,256]{1,0:T(8,128)(2,1)}, bf16[1024,256]{1,0:T(8,128)(2,1)}, bf16[1024,256]{1,0:T(8,128)(2,1)}, f32[1024,256]{1,0:T(8,128)}) custom-call(bf16[1024,256]{1,0:T(8,128)(2,1)} %get-tuple-element.8.q_ref, bf16[1024,256]{1,0:T(8,128)(2,1)} %get-tuple-element.9.k_ref, bf16[1024,256]{1,0:T(8,128)(2,1)} %get-tuple-element.10.v_ref, ...), custom_call_target="tpu_custom_call" | custom-call | tf_op jit(solution)/shard_map/store_grads/pallas_call | solution.py:274

commit v3 on v2

--- a/solution.py
+++ b/solution.py
@@ -45,79 +45,129 @@
     k_hbm, v_hbm, g_hbm, q_hbm, taps_hbm, skip_hbm, first_hbm, last_hbm, twist_hbm, forth_hbm, back_hbm,
     q_hbm_out, k_hbm_out, v_hbm_out, tap_out,
     q_out, k_out, v_out, k_in, v_in, g_in, q_in, taps_in, skip_in, first, last, twist, forth, back,
-    sent, arrived, returned, packed, wide, gated_spec, taps_spec, prod_spec, mixed,
-    load_sem, store_sem, own_sem, send_sem, recv_sem,
+    sent, crossed, arrived, returned, packed, wide, gated_spec, taps_spec, prod_spec, mixed,
+    load_sem, store_sem, own_sem, ready, cross_send, cross_recv, plane_send, plane_recv,
 ):
     me = lax.axis_index("ctx")
+    half = blocks // 2
+    z = lax.rem(lax.div(me, 2), 2)
+    i = 2 * lax.div(me, 4) + lax.rem(me, 2)
+    partner = me + 2 - 4 * z
     rows = blocks * count
+    side = half * count
     lanes = 128
     halves = width // lanes
     loads = [
-        pltpu.make_async_copy(src, dst, load_sem.at[i])
-        for i, (src, dst) in enumerate(
+        pltpu.make_async_copy(src, dst, load_sem.at[n])
+        for n, (src, dst) in enumerate(
             (
                 (k_hbm, k_in), (v_hbm, v_in), (taps_hbm, taps_in), (g_hbm, g_in), (q_hbm, q_in),
                 (skip_hbm, skip_in), (first_hbm, first), (last_hbm, last), (twist_hbm, twist), (forth_hbm, forth), (back_hbm, back),
             )
         )
     ]
-    for load in loads:
+    for load in loads[:2]:
         load.start()
 
+    def block(index):
+        return pl.ds(pl.multiple_of(index * count, count), count)
+
+    def part_of(which):
+        return pl.ds(pl.multiple_of(which * side, side), side)
+
+    def plane_device(k):
+        place = lax.rem(i + k, half)
+        return place, 4 * lax.div(place, 2) + 2 * z + lax.rem(place, 2)
+
     barrier = pltpu.get_barrier_semaphore()
-
-    def greet(j, carry):
-        peer = lax.rem(me + j, blocks)
+    pl.semaphore_signal(barrier, inc=1, device_id={"ctx": partner}, device_id_type=MESH)
+
+    def greet(k, carry):
+        _, peer = plane_device(k)
         pl.semaphore_signal(barrier, inc=1, device_id={"ctx": peer}, device_id_type=MESH)
         return carry
 
-    lax.fori_loop(1, blocks, greet, 0)
-
-    def own_rows():
-        return pl.ds(pl.multiple_of(me * count, count), count)
-
-    def send(i, target):
-        def one(j, carry):
-            peer = lax.rem(me + j, blocks)
+    lax.fori_loop(1, half, greet, 0)
+    for load in loads[2:]:
+        load.start()
+
+    def cross(src, dst):
+        pltpu.make_async_remote_copy(
+            src_ref=src, dst_ref=dst, send_sem=cross_send, recv_sem=cross_recv,
+            device_id={"ctx": partner}, device_id_type=MESH,
+        ).start()
+
+    def in_plane(n, moves):
+        def one(k, carry):
+            place, peer = plane_device(k)
+            for slot, src, dst in moves(place, peer):
+                pltpu.make_async_remote_copy(
+                    src_ref=src, dst_ref=dst, send_sem=plane_send.at[n], recv_sem=plane_recv.at[slot],
+                    device_id={"ctx": peer}, device_id_type=MESH,
+                ).start()
+            return carry
+
+        lax.fori_loop(1, half, one, 0)
+
+    def wait_rows(ref, n_rows, sem):
+        part = ref.at[pl.ds(0, n_rows)]
+        pltpu.make_async_copy(part, part, sem).wait()
+
+    def send_own(n):
+        in_plane(n, lambda place, peer: [(n, sent.at[n, block(z * half + place)], arrived.at[n, block(me)])])
+        arrived[n, block(me)] = sent[n, block(z * half + i)]
+
+    def send_on(n):
+        wait_rows(crossed, side, cross_recv)
+        in_plane(n, lambda place, peer: [(n, crossed.at[block(place)], arrived.at[n, block(partner)])])
+        arrived[n, block(partner)] = crossed[block(i)]
+
+    def to_all(n, recv, source, dst):
+        def one(k, carry):
+            peer = lax.rem(me + k, blocks)
             pltpu.make_async_remote_copy(
-                src_ref=sent.at[i, pl.ds(pl.multiple_of(peer * count, count), count)],
-                dst_ref=target.at[own_rows()],
-                send_sem=send_sem.at[i],
-                recv_sem=recv_sem.at[i],
-                device_id={"ctx": peer},
-                device_id_type=MESH,
+                src_ref=source(peer), dst_ref=dst, send_sem=plane_send.at[n], recv_sem=plane_recv.at[recv],
+                device_id={"ctx": peer}, device_id_type=MESH,
             ).start()
             return carry
 
         lax.fori_loop(1, blocks, one, 0)
 
-    def wait_all(i, target, sem):
-        part = pl.ds(0, rows - count)
-        pltpu.make_async_copy(target.at[part], target.at[part], sem.at[i]).wait()
+    def owner_block(device):
+        return block(lax.rem(lax.div(device, 2), 2) * half + 2 * lax.div(device, 4) + lax.rem(device, 2))
+
+    def send_direct(n):
+        to_all(n, n, lambda peer: sent.at[n, owner_block(peer)], arrived.at[n, block(me)])
+        arrived[n, block(me)] = sent[n, owner_block(me)]
+
+    def give(n, target):
+        to_all(n, n, lambda peer: sent.at[n, block(peer)], target.at[owner_block(me)])
 
     loads[0].wait()
     loads[1].wait()
     sent[0] = (k_in[...].astype(F32) * v_in[...].astype(F32)).astype(BF16)
-    pl.semaphore_wait(barrier, blocks - 1)
-    send(0, arrived.at[0])
+    pl.semaphore_wait(barrier, half)
+    cross(sent.at[0, part_of(1 - z)], crossed)
+    pl.semaphore_signal(ready, inc=1, device_id={"ctx": partner}, device_id_type=MESH)
+    send_own(0)
     loads[2].wait()
     sent[1] = taps_in[...].astype(BF16)
-    send(1, arrived.at[1])
     loads[3].wait()
     loads[4].wait()
     sent[2] = (g_in[...].astype(F32) * q_in[...].astype(F32)).astype(BF16)
-    send(2, arrived.at[2])
+    pl.semaphore_wait(ready, 1)
+    send_direct(1)
+    send_direct(2)
     for load in loads[5:]:
         load.wait()
 
     group = 4
     tile = group * blocks
 
-    def transform(i, spec):
-        wait_all(i, arrived.at[i], recv_sem)
-        arrived[i, own_rows()] = sent[i, own_rows()]
+    def transform(n, spec):
+        wait_rows(arrived.at[n], rows - (2 if n == 0 else 1) * count, plane_recv.at[n])
         for h in range(halves):
-            wide[h] = arrived[i, :, lanes * h : lanes * (h + 1)].astype(F32)
+            wide[h] = arrived[n, :, lanes * h : lanes * (h + 1)].astype(F32)
 
         def one(t, carry):
             for s in range(group):
@@ -133,7 +183,7 @@
 
         lax.fori_loop(0, count // group, one, 0)
 
-    def multiply_back(i, left, right, conjugate, scale):
+    def multiply_back(n, left, right, conjugate, scale):
         def one(t, carry):
             part = pl.ds(pl.multiple_of(t * tile, tile), tile)
             lr, li = left[part, :width], left[part, width:]
@@ -159,25 +209,24 @@
 
         lax.fori_loop(0, count // group, one, 0)
         for h in range(halves):
-            sent[i, :, lanes * h : lanes * (h + 1)] = wide[h].astype(BF16)
-
-    def give(i, target):
-        send(i, target)
-        target[own_rows()] = sent[i, own_rows()]
+            sent[n, :, lanes * h : lanes * (h + 1)] = wide[h].astype(BF16)
 
     norm = 1.0 / (blocks * width)
     fwd, bwd = returned.at[0], returned.at[1]
+    send_on(0)
     transform(0, gated_spec)
     transform(1, taps_spec)
     multiply_back(3, gated_spec, taps_spec, False, norm)
     give(3, fwd)
+    fwd[owner_block(me)] = sent[3, block(me)]
     transform(2, prod_spec)
     multiply_back(4, prod_spec, taps_spec, True, norm)
     give(4, bwd)
+    bwd[owner_block(me)] = sent[4, block(me)]
     multiply_back(5, prod_spec, gated_spec, True, norm * (blocks * width) ** -0.5)
-    own_taps = pltpu.make_async_copy(sent.at[5, own_rows()], tap_out.at[own_rows()], own_sem)
+    give(5, tap_out)
+    own_taps = pltpu.make_async_copy(sent.at[5, block(me)], tap_out.at[owner_block(me)], own_sem)
     own_taps.start()
-    send(5, tap_out)
 
     skip_cols = skip_in[...].T
 
@@ -195,22 +244,23 @@
         v_out[part] = (k_in[part].astype(F32) * z_grad).astype(BF16)
 
     stores = [
-        pltpu.make_async_copy(src, dst, store_sem.at[i])
-        for i, (src, dst) in enumerate(((q_out, q_hbm_out), (k_out, k_hbm_out), (v_out, v_hbm_out)))
+        pltpu.make_async_copy(src, dst, store_sem.at[n])
+        for n, (src, dst) in enumerate(((q_out, q_hbm_out), (k_out, k_hbm_out), (v_out, v_hbm_out)))
     ]
-    wait_all(3, fwd, recv_sem)
+    wait_rows(fwd, rows - count, plane_recv.at[3])
     each_part(finish_q)
     stores[0].start()
-    wait_all(4, bwd, recv_sem)
+    wait_rows(bwd, rows - count, plane_recv.at[4])
     each_part(finish_kv)
     stores[1].start()
     stores[2].start()
     own_taps.wait()
     for store in stores:
         store.wait()
-    for i in range(6):
-        wait_all(i, sent.at[i], send_sem)
-    wait_all(5, tap_out, recv_sem)
+    wait_rows(crossed, side, cross_send)
+    for n in range(6):
+        wait_rows(sent.at[n], rows - (2 if n == 0 else 1) * count, plane_send.at[n])
+    wait_rows(tap_out, rows - count, plane_recv.at[5])
 
 
 def store_kernel(q_ref, k_ref, v_ref, tap_ref, q_out, k_out, v_out, tap_out, held, wide, sems):
@@ -255,13 +305,14 @@
             field, field, field, field, field, field, field,
             pltpu.VMEM((rows, width), F32), pltpu.VMEM((rows // lanes, lanes), F32), *table_space,
             pltpu.VMEM((6, rows, width), BF16),
+            pltpu.VMEM((rows // 2, width), BF16),
             pltpu.VMEM((3, rows, width), BF16),
             pltpu.VMEM((2, rows, width), BF16),
             pltpu.VMEM((4 * blocks, 2 * width), BF16),
             pltpu.VMEM((width // lanes, rows, lanes), F32),
             spectrum, spectrum, spectrum,
             pltpu.VMEM((4 * blocks, 2 * width), BF16),
-            dma((11,)), dma((3,)), dma, dma((6,)), dma((6,)),
+            dma((11,)), dma((3,)), dma, pltpu.SemaphoreType.REGULAR, dma, dma, dma((6,)), dma((6,)),
         ],
         compiler_params=pltpu.CompilerParams(
             collective_id=0, has_side_effects=True, vmem_limit_bytes=58 * 2**20

time: 87.9 us -> 86.6 us (0.985)
  the two profiles are of different devices: /device:TPU:65 before, /device:TPU:1 now
where the time goes in v3:
time: 86.6 us; the launch traced here: 85.1 us
  Pallas kernels  84.5 us (98%)
    pallas_call x1, Pallas kernels, exchange_convolve(): pl.pallas_call(functools.partial(kernel, blocks, count, width), out_shape...  81.9 us
    pallas_call x1, Pallas kernels, exchange_convolve(): pl.pallas_call(store_kernel, out_shape=[result] * 3 + [jax.ShapeDtypeStru...  2.6 us

profile of v3, /device:TPU:1, one launch (start us, length us, event | category | flops | bytes accessed | tf_op | source)
XLA Modules:
  0.0 85.1 jit_solution(13582255417584057519)
XLA Ops:
  0.6 81.9 %exchange_convolve.1 = (bf16[1024,256]{1,0:T(8,128)(2,1)}, bf16[1024,256]{1,0:T(8,128)(2,1)}, bf16[1024,256]{1,0:T(8,128)(2,1)}, bf16[1024,256]{1,0:T(8,128)(2,1)}) custom-call(bf16[1024,256]{1,0:T(8,128)(2,1)} %k_hbm.1, bf16[1024,256]{1,0:T(8,128)(2,1)} %v_hbm.1, bf16[1024,256]{1,0:T(8,128)(2,1)} %g_hbm.1, bf16[1024,256]{1,0:T(8,128)(2,1)} %q_hbm.1, ...), custom_call_target="tpu_custom_call" | custom-call | tf_op jit(solution)/shard_map/exchange_convolve/pallas_call | solution.py:299
  82.5 2.6 %store_grads.1 = (bf16[1024,256]{1,0:T(8,128)(2,1)}, bf16[1024,256]{1,0:T(8,128)(2,1)}, bf16[1024,256]{1,0:T(8,128)(2,1)}, f32[1024,256]{1,0:T(8,128)}) custom-call(bf16[1024,256]{1,0:T(8,128)(2,1)} %get-tuple-element.8.q_ref, bf16[1024,256]{1,0:T(8,128)(2,1)} %get-tuple-element.9.k_ref, bf16[1024,256]{1,0:T(8,128)(2,1)} %get-tuple-element.10.v_ref, ...), custom_call_target="tpu_custom_call" | custom-call | tf_op jit(solution)/shard_map/store_grads/pallas_call | solution.py:325

commit v4 on v3

--- a/solution.py
+++ b/solution.py
@@ -14,30 +14,41 @@
 F32 = jnp.float32
 
 
-def split_table(table, axis):
+def split_table(table):
     high = table.astype(ml_dtypes.bfloat16)
-    low = (table - high.astype(np.float64)).astype(ml_dtypes.bfloat16)
-    return np.concatenate([high, low], axis=axis)
+    return high, (table - high.astype(np.float64)).astype(ml_dtypes.bfloat16)
+
+
+def split(x):
+    high = x.astype(BF16)
+    return high, (x - high.astype(F32)).astype(BF16)
 
 
 def make_tables(blocks, width):
     a = np.arange(blocks)[:, None]
     c = np.arange(blocks)[None, :] + 0.5
     phase = 2 * np.pi * a * c / (2 * blocks)
-    first = split_table(np.concatenate([np.cos(phase).T, -np.sin(phase).T], axis=0), 1)
-    last = split_table(np.concatenate([np.cos(phase), -np.sin(phase)], axis=1), 1)
+    first = np.concatenate(split_table(np.concatenate([np.cos(phase).T, -np.sin(phase).T], axis=0)), axis=1)
+    high, low = split_table(np.concatenate([np.cos(phase), -np.sin(phase)], axis=1))
+    last = np.concatenate([high, low, high], axis=1)
     b = np.arange(width)
     turn = 2 * np.pi * c.T * b[None, :] / (2 * blocks * width)
     twist = np.concatenate([np.cos(turn), np.sin(turn)], axis=0).astype(np.float32)
     angle = 2 * np.pi * ((b[:, None] * b[None, :]) % width) / width
     cos, sin = np.cos(angle), np.sin(angle)
-    forth = np.block([[cos, -sin], [sin, cos]]).astype(ml_dtypes.bfloat16)
-    back = np.block([[cos, sin], [-sin, cos]]).astype(ml_dtypes.bfloat16)
+    forth = np.stack(split_table(np.block([[cos, -sin], [sin, cos]])))
+    back = np.stack(split_table(np.block([[cos, sin], [-sin, cos]])))
     return first, last, twist, forth, back
 
 
 def dot(x, y):
     return jnp.dot(x, y, preferred_element_type=F32)
+
+
+def dot_split(x, table):
+    return dot(
+        jnp.concatenate([x[0], x[0], x[1]], axis=1), jnp.concatenate([table[0], table[1], table[0]], axis=0)
+    )
 
 
 def kernel(
@@ -176,9 +187,10 @@
                 y = dot(first[...], jnp.concatenate([x, x], axis=0))
                 real, imag = y[:blocks], y[blocks:]
                 cos, sin = twist[:blocks], twist[blocks:]
-                packed[s * blocks : (s + 1) * blocks, :width] = (real * cos + imag * sin).astype(BF16)
-                packed[s * blocks : (s + 1) * blocks, width:] = (imag * cos - real * sin).astype(BF16)
-            spec[pl.ds(pl.multiple_of(t * tile, tile), tile), :] = dot(packed[...], forth[...])
+                part = slice(s * blocks, (s + 1) * blocks)
+                packed[0, part, :width], packed[1, part, :width] = split(real * cos + imag * sin)
+                packed[0, part, width:], packed[1, part, width:] = split(imag * cos - real * sin)
+            spec[pl.ds(pl.multiple_of(t * tile, tile), tile), :] = dot_split(packed, forth)
             return carry
 
         lax.fori_loop(0, count // group, one, 0)
@@ -189,20 +201,18 @@
             lr, li = left[part, :width], left[part, width:]
             rr, ri = right[part, :width], right[part, width:]
             if conjugate:
-                mixed[:, :width] = (lr * rr + li * ri).astype(BF16)
-                mixed[:, width:] = (li * rr - lr * ri).astype(BF16)
+                mixed[0, :, :width], mixed[1, :, :width] = split(lr * rr + li * ri)
+                mixed[0, :, width:], mixed[1, :, width:] = split(li * rr - lr * ri)
             else:
-                mixed[:, :width] = (lr * rr - li * ri).astype(BF16)
-                mixed[:, width:] = (lr * ri + li * rr).astype(BF16)
-            u = dot(mixed[...], back[...])
+                mixed[0, :, :width], mixed[1, :, :width] = split(lr * rr - li * ri)
+                mixed[0, :, width:], mixed[1, :, width:] = split(lr * ri + li * rr)
+            u = dot_split(mixed, back)
             cos, sin = twist[:blocks] * scale, twist[blocks:] * scale
             for s in range(group):
                 real = u[s * blocks : (s + 1) * blocks, :width]
                 imag = u[s * blocks : (s + 1) * blocks, width:]
-                turned = jnp.concatenate(
-                    [(real * cos - imag * sin).astype(BF16), (imag * cos + real * sin).astype(BF16)], axis=0
-                )
-                out = dot(last[...], jnp.concatenate([turned, turned], axis=0))
+                high, low = split(jnp.concatenate([real * cos - imag * sin, imag * cos + real * sin], axis=0))
+                out = dot(last[...], jnp.concatenate([high, high, low], axis=0))
                 for h in range(halves):
                     wide[h, pl.ds(t * group + s, blocks, stride=count), :] = out[:, lanes * h : lanes * (h + 1)]
             return carry
@@ -308,10 +318,10 @@
             pltpu.VMEM((rows // 2, width), BF16),
             pltpu.VMEM((3, rows, width), BF16),
             pltpu.VMEM((2, rows, width), BF16),
-            pltpu.VMEM((4 * blocks, 2 * width), BF16),
+            pltpu.VMEM((2, 4 * blocks, 2 * width), BF16),
             pltpu.VMEM((width // lanes, rows, lanes), F32),
             spectrum, spectrum, spectrum,
-            pltpu.VMEM((4 * blocks, 2 * width), BF16),
+            pltpu.VMEM((2, 4 * blocks, 2 * width), BF16),
             dma((11,)), dma((3,)), dma, pltpu.SemaphoreType.REGULAR, dma, dma, dma((6,)), dma((6,)),
         ],
         compiler_params=pltpu.CompilerParams(

time: 86.6 us -> 88.3 us (1.020); the launches traced: 85.1 us -> 88.2 us
  Pallas kernels: 84.5 us -> 87.5 us
    pallas_call x1, Pallas kernels: 81.9 us -> 84.9 us  [exchange_convolve(): pl.pallas_call(functools.partial(kernel, blocks, count, width), out_shape...]
where the time goes in v4:
time: 88.3 us; the launch traced here: 88.2 us
  Pallas kernels  87.5 us (99%)
    pallas_call x1, Pallas kernels, exchange_convolve(): pl.pallas_call(functools.partial(kernel, blocks, count, width), out_shape...  84.9 us
    pallas_call x1, Pallas kernels, exchange_convolve(): pl.pallas_call(store_kernel, out_shape=[result] * 3 + [jax.ShapeDtypeStru...  2.6 us

profile of v4, /device:TPU:1, one launch (start us, length us, event | category | flops | bytes accessed | tf_op | source)
XLA Modules:
  0.0 88.2 jit_solution(7814991564423971560)
XLA Ops:
  0.6 84.9 %exchange_convolve.1 = (bf16[1024,256]{1,0:T(8,128)(2,1)}, bf16[1024,256]{1,0:T(8,128)(2,1)}, bf16[1024,256]{1,0:T(8,128)(2,1)}, bf16[1024,256]{1,0:T(8,128)(2,1)}) custom-call(bf16[1024,256]{1,0:T(8,128)(2,1)} %k_hbm.1, bf16[1024,256]{1,0:T(8,128)(2,1)} %v_hbm.1, bf16[1024,256]{1,0:T(8,128)(2,1)} %g_hbm.1, bf16[1024,256]{1,0:T(8,128)(2,1)} %q_hbm.1, ...), custom_call_target="tpu_custom_call" | custom-call | tf_op jit(solution)/shard_map/exchange_convolve/pallas_call | solution.py:309
  85.6 2.6 %store_grads.1 = (bf16[1024,256]{1,0:T(8,128)(2,1)}, bf16[1024,256]{1,0:T(8,128)(2,1)}, bf16[1024,256]{1,0:T(8,128)(2,1)}, f32[1024,256]{1,0:T(8,128)}) custom-call(bf16[1024,256]{1,0:T(8,128)(2,1)} %get-tuple-element.8.q_ref, bf16[1024,256]{1,0:T(8,128)(2,1)} %get-tuple-element.9.k_ref, bf16[1024,256]{1,0:T(8,128)(2,1)} %get-tuple-element.10.v_ref, ...), custom_call_target="tpu_custom_call" | custom-call | tf_op jit(solution)/shard_map/store_grads/pallas_call | solution.py:335

commit v5 on v4

--- a/solution.py
+++ b/solution.py
@@ -160,7 +160,6 @@
     pl.semaphore_wait(barrier, half)
     cross(sent.at[0, part_of(1 - z)], crossed)
     pl.semaphore_signal(ready, inc=1, device_id={"ctx": partner}, device_id_type=MESH)
-    send_own(0)
     loads[2].wait()
     sent[1] = taps_in[...].astype(BF16)
     loads[3].wait()
@@ -168,6 +167,7 @@
     sent[2] = (g_in[...].astype(F32) * q_in[...].astype(F32)).astype(BF16)
     pl.semaphore_wait(ready, 1)
     send_direct(1)
+    send_own(0)
     send_direct(2)
     for load in loads[5:]:
         load.wait()
@@ -180,7 +180,8 @@
         for h in range(halves):
             wide[h] = arrived[n, :, lanes * h : lanes * (h + 1)].astype(F32)
 
-        def one(t, carry):
+        for t in range(count // group):
+            held = packed.at[t]
             for s in range(group):
                 every = pl.ds(t * group + s, blocks, stride=count)
                 x = jnp.concatenate([wide[h, every, :] for h in range(halves)], axis=1).astype(BF16)
@@ -188,25 +189,23 @@
                 real, imag = y[:blocks], y[blocks:]
                 cos, sin = twist[:blocks], twist[blocks:]
                 part = slice(s * blocks, (s + 1) * blocks)
-                packed[0, part, :width], packed[1, part, :width] = split(real * cos + imag * sin)
-                packed[0, part, width:], packed[1, part, width:] = split(imag * cos - real * sin)
-            spec[pl.ds(pl.multiple_of(t * tile, tile), tile), :] = dot_split(packed, forth)
-            return carry
-
-        lax.fori_loop(0, count // group, one, 0)
+                held[0, part, :width], held[1, part, :width] = split(real * cos + imag * sin)
+                held[0, part, width:], held[1, part, width:] = split(imag * cos - real * sin)
+            spec[t * tile : (t + 1) * tile, :] = dot_split(held, forth)
 
     def multiply_back(n, left, right, conjugate, scale):
-        def one(t, carry):
-            part = pl.ds(pl.multiple_of(t * tile, tile), tile)
+        for t in range(count // group):
+            held = mixed.at[t]
+            part = slice(t * tile, (t + 1) * tile)
             lr, li = left[part, :width], left[part, width:]
             rr, ri = right[part, :width], right[part, width:]
             if conjugate:
-                mixed[0, :, :width], mixed[1, :, :width] = split(lr * rr + li * ri)
-                mixed[0, :, width:], mixed[1, :, width:] = split(li * rr - lr * ri)
+                held[0, :, :width], held[1, :, :width] = split(lr * rr + li * ri)
+                held[0, :, width:], held[1, :, width:] = split(li * rr - lr * ri)
             else:
-                mixed[0, :, :width], mixed[1, :, :width] = split(lr * rr - li * ri)
-                mixed[0, :, width:], mixed[1, :, width:] = split(lr * ri + li * rr)
-            u = dot_split(mixed, back)
+                held[0, :, :width], held[1, :, :width] = split(lr * rr - li * ri)
+                held[0, :, width:], held[1, :, width:] = split(lr * ri + li * rr)
+            u = dot_split(held, back)
             cos, sin = twist[:blocks] * scale, twist[blocks:] * scale
             for s in range(group):
                 real = u[s * blocks : (s + 1) * blocks, :width]
@@ -215,9 +214,6 @@
                 out = dot(last[...], jnp.concatenate([high, high, low], axis=0))
                 for h in range(halves):
                     wide[h, pl.ds(t * group + s, blocks, stride=count), :] = out[:, lanes * h : lanes * (h + 1)]
-            return carry
-
-        lax.fori_loop(0, count // group, one, 0)
         for h in range(halves):
             sent[n, :, lanes * h : lanes * (h + 1)] = wide[h].astype(BF16)
 
@@ -318,10 +314,10 @@
             pltpu.VMEM((rows // 2, width), BF16),
             pltpu.VMEM((3, rows, width), BF16),
             pltpu.VMEM((2, rows, width), BF16),
-            pltpu.VMEM((2, 4 * blocks, 2 * width), BF16),
+            pltpu.VMEM((count // 4, 2, 4 * blocks, 2 * width), BF16),
             pltpu.VMEM((width // lanes, rows, lanes), F32),
             spectrum, spectrum, spectrum,
-            pltpu.VMEM((2, 4 * blocks, 2 * width), BF16),
+            pltpu.VMEM((count // 4, 2, 4 * blocks, 2 * width), BF16),
             dma((11,)), dma((3,)), dma, pltpu.SemaphoreType.REGULAR, dma, dma, dma((6,)), dma((6,)),
         ],
         compiler_params=pltpu.CompilerParams(

time: 88.3 us -> 87.5 us (level)
  Pallas kernels: 87.5 us -> 86.6 us
    pallas_call x1, Pallas kernels: 84.9 us -> 84 us  [exchange_convolve(): pl.pallas_call(functools.partial(kernel, blocks, count, width), out_shape...]
where the time goes in v5:
time: 87.5 us; the launch traced here: 87.4 us
  Pallas kernels  86.6 us (99%)
    pallas_call x1, Pallas kernels, exchange_convolve(): pl.pallas_call(functools.partial(kernel, blocks, count, width), out_shape...  84 us
    pallas_call x1, Pallas kernels, exchange_convolve(): pl.pallas_call(store_kernel, out_shape=[result] * 3 + [jax.ShapeDtypeStru...  2.6 us

profile of v5, /device:TPU:1, one launch (start us, length us, event | category | flops | bytes accessed | tf_op | source)
XLA Modules:
  0.0 87.4 jit_solution(5542883068505820957)
XLA Ops:
  0.6 84.0 %exchange_convolve.1 = (bf16[1024,256]{1,0:T(8,128)(2,1)}, bf16[1024,256]{1,0:T(8,128)(2,1)}, bf16[1024,256]{1,0:T(8,128)(2,1)}, bf16[1024,256]{1,0:T(8,128)(2,1)}) custom-call(bf16[1024,256]{1,0:T(8,128)(2,1)} %k_hbm.1, bf16[1024,256]{1,0:T(8,128)(2,1)} %v_hbm.1, bf16[1024,256]{1,0:T(8,128)(2,1)} %g_hbm.1, bf16[1024,256]{1,0:T(8,128)(2,1)} %q_hbm.1, ...), custom_call_target="tpu_custom_call" | custom-call | tf_op jit(solution)/shard_map/exchange_convolve/pallas_call | solution.py:305
  84.6 2.6 %store_grads.1 = (bf16[1024,256]{1,0:T(8,128)(2,1)}, bf16[1024,256]{1,0:T(8,128)(2,1)}, bf16[1024,256]{1,0:T(8,128)(2,1)}, f32[1024,256]{1,0:T(8,128)}) custom-call(bf16[1024,256]{1,0:T(8,128)(2,1)} %get-tuple-element.8.q_ref, bf16[1024,256]{1,0:T(8,128)(2,1)} %get-tuple-element.9.k_ref, bf16[1024,256]{1,0:T(8,128)(2,1)} %get-tuple-element.10.v_ref, ...), custom_call_target="tpu_custom_call" | custom-call | tf_op jit(solution)/shard_map/store_grads/pallas_call | solution.py:331

commit v6 on v5

--- a/solution.py
+++ b/solution.py
@@ -158,8 +158,8 @@
     loads[1].wait()
     sent[0] = (k_in[...].astype(F32) * v_in[...].astype(F32)).astype(BF16)
     pl.semaphore_wait(barrier, half)
+    pl.semaphore_signal(ready, inc=1, device_id={"ctx": partner}, device_id_type=MESH)
     cross(sent.at[0, part_of(1 - z)], crossed)
-    pl.semaphore_signal(ready, inc=1, device_id={"ctx": partner}, device_id_type=MESH)
     loads[2].wait()
     sent[1] = taps_in[...].astype(BF16)
     loads[3].wait()

time: 87.5 us -> 87.5 us (level)
  no operation moved by 1% of the time
where the time goes in v6:
time: 87.5 us; the launch traced here: 87.4 us
  Pallas kernels  86.6 us (99%)
    pallas_call x1, Pallas kernels, exchange_convolve(): pl.pallas_call(functools.partial(kernel, blocks, count, width), out_shape...  84 us
    pallas_call x1, Pallas kernels, exchange_convolve(): pl.pallas_call(store_kernel, out_shape=[result] * 3 + [jax.ShapeDtypeStru...  2.6 us

profile of v6, /device:TPU:1, one launch (start us, length us, event | category | flops | bytes accessed | tf_op | source)
XLA Modules:
  0.0 87.4 jit_solution(4343970462255630183)
XLA Ops:
  0.6 84.0 %exchange_convolve.1 = (bf16[1024,256]{1,0:T(8,128)(2,1)}, bf16[1024,256]{1,0:T(8,128)(2,1)}, bf16[1024,256]{1,0:T(8,128)(2,1)}, bf16[1024,256]{1,0:T(8,128)(2,1)}) custom-call(bf16[1024,256]{1,0:T(8,128)(2,1)} %k_hbm.1, bf16[1024,256]{1,0:T(8,128)(2,1)} %v_hbm.1, bf16[1024,256]{1,0:T(8,128)(2,1)} %g_hbm.1, bf16[1024,256]{1,0:T(8,128)(2,1)} %q_hbm.1, ...), custom_call_target="tpu_custom_call" | custom-call | tf_op jit(solution)/shard_map/exchange_convolve/pallas_call | solution.py:305
  84.7 2.6 %store_grads.1 = (bf16[1024,256]{1,0:T(8,128)(2,1)}, bf16[1024,256]{1,0:T(8,128)(2,1)}, bf16[1024,256]{1,0:T(8,128)(2,1)}, f32[1024,256]{1,0:T(8,128)}) custom-call(bf16[1024,256]{1,0:T(8,128)(2,1)} %get-tuple-element.8.q_ref, bf16[1024,256]{1,0:T(8,128)(2,1)} %get-tuple-element.9.k_ref, bf16[1024,256]{1,0:T(8,128)(2,1)} %get-tuple-element.10.v_ref, ...), custom_call_target="tpu_custom_call" | custom-call | tf_op jit(solution)/shard_map/store_grads/pallas_call | solution.py:331
